TPU v7x, 32 devices: a whole 2x2x4 slice. The times are simulated.
32 devices in a mesh: groups: 2 (over y), units: 8 (over z, core), cuts: 2 (over x).
Axes of the slice: x: 2, y: 2, z: 4, core: 2. Of those that a mesh axis runs over, the one named last changes fastest.
Arguments:
- residual: bfloat16 [256, 6144], P('groups', 'units'), parts along dimension 0, may hold values from -6 to 6
- query: bfloat16 [256, 6144], P(('groups', 'units'), 'cuts'), parts along dimension 0, may hold values from -48 to 48
- key_cache: bfloat16 [256, 512, 1024], P(('groups', 'units'), None, 'cuts'), parts along dimension 0, may hold values from -8 to 8
- value_cache: bfloat16 [256, 512, 1024], P(('groups', 'units'), None, 'cuts'), parts along dimension 0, may hold values from -7 to 7
- new_key: bfloat16 [256, 1024], P(('groups', 'units'), 'cuts'), parts along dimension 0, may hold values from -8 to 8
- new_value: bfloat16 [256, 1024], P(('groups', 'units'), 'cuts'), parts along dimension 0, may hold values from -6 to 6
- lengths: int32 [256], P(('groups', 'units')), parts along dimension 0, may hold values from 1 to 512, 32768 in all
- out_weight: bfloat16 [6144, 6144], P('cuts', 'units'), may hold values from -1 to 1
- router_weight: float32 [6144, 4], P('units'), may hold values from -0.078125 to 0.078125
- norm_gain: float32 [6144], P('units'), may hold values from 0.5 to 1.5
- expert_ids: int32 [256, 2], P('groups'), parts along dimension 0, may hold values from 0 to 3, all different within a row; in each aligned block of 128 rows (0 to 127, 128 to 255, ...) at most 80 rows name the same one
- gate_weight: bfloat16 [6144, 32768], P(None, ('units', 'cuts')), may hold values from -0.078125 to 0.078125
- up_weight: bfloat16 [6144, 32768], P(None, ('units', 'cuts')), may hold values from -0.078125 to 0.078125
- down_weight: bfloat16 [32768, 6144], P(('units', 'cuts')), may hold values from -0.1875 to 0.1875
Outputs:
- mixed: bfloat16 [256, 6144], P('groups', 'units'), parts along dimension 0
There are 2 independent parts, one for each index of `groups`. A program takes and returns all parts, laid end to end along the dimension named above; an argument that names none is the same for every part. Nothing has to cross between parts.
Inputs may be any that keep to these rules, and one draw needn't show every extreme that they name: `expert_ids`: each row names two different experts; no expert is named by more than 80 rows, and one is named by exactly 80.
All inputs are finite; a program needn't handle non-finite values. No bound on the sum of `lengths` on one device may be relied on, other than what follows from the above.
Results may differ from a plain program's by a relative error of at most 0.013.
Values may be sent and summed in bfloat16 or wider, within the bound.
A program may use at most 192 MiB of HBM per device.

v0:
```python
import jax
import jax.numpy as jnp
from jax import lax
from jax.sharding import PartitionSpec as P

D = 6144
HD = 128
EXPERTS = 4


eps = 1e-05


def attend(query, key_cache, value_cache, new_key, new_value, lengths):
    row_count = query.shape[0]
    slot_count = key_cache.shape[1]
    kv_local = key_cache.shape[2] // HD
    share = query.shape[1] // HD // kv_local
    scale_factor = HD ** (-0.5)
    q_heads = query.reshape(row_count, kv_local, share, HD)
    keys_all = key_cache.reshape(row_count, slot_count, kv_local, HD)
    values_all = value_cache.reshape(row_count, slot_count, kv_local, HD)
    key_own = new_key.reshape(row_count, kv_local, HD)
    value_own = new_value.reshape(row_count, kv_local, HD)
    scores = (
        jnp.einsum("rkgd,rtkd->rkgt", q_heads, keys_all, preferred_element_type=jnp.float32)
        * scale_factor
    )
    valid = (jnp.arange(slot_count, dtype=jnp.int32)[None, :] < lengths[:, None])[:, None, None, :]
    scores = jnp.where(valid, scores, -jnp.inf)
    own_score = (
        jnp.einsum("rkgd,rkd->rkg", q_heads, key_own, preferred_element_type=jnp.float32)
        * scale_factor
    )
    highest = jnp.maximum(jnp.max(scores, axis=-1), own_score)
    weights = jnp.exp(scores - highest[..., None])
    own_weight = jnp.exp(own_score - highest)
    total = jnp.sum(weights, axis=-1) + own_weight
    probs = (weights / total[..., None]).astype(jnp.bfloat16)
    own_prob = (own_weight / total).astype(jnp.bfloat16)
    heads_out = jnp.einsum("rkgt,rtkd->rkgd", probs, values_all, preferred_element_type=jnp.float32)
    heads_out = (
        heads_out
        + own_prob.astype(jnp.float32)[..., None] * value_own.astype(jnp.float32)[:, :, None, :]
    )
    return heads_out.reshape(row_count, kv_local * share * HD).astype(jnp.bfloat16)


def expert_block(rows_in, gate_weight, up_weight, down_weight):
    gate_part = jnp.dot(rows_in, gate_weight, preferred_element_type=jnp.float32)
    up_part = jnp.dot(rows_in, up_weight, preferred_element_type=jnp.float32)
    inner = (jax.nn.silu(gate_part) * up_part).astype(jnp.bfloat16)
    return jnp.dot(inner, down_weight, preferred_element_type=jnp.float32)


def shards(
    residual,
    query,
    key_cache,
    value_cache,
    new_key,
    new_value,
    lengths,
    out_weight,
    router_weight,
    norm_gain,
    expert_ids,
    gate_weight,
    up_weight,
    down_weight,
):
    attended = attend(query, key_cache, value_cache, new_key, new_value, lengths)
    partial_out = jnp.dot(
        lax.all_gather(attended, "units", axis=0, tiled=True),
        out_weight,
        preferred_element_type=jnp.float32,
    )
    projected = lax.psum(partial_out, "cuts")
    hidden_state = residual.astype(jnp.float32) + projected
    scaled = hidden_state * norm_gain
    local_squares = jnp.sum(hidden_state * hidden_state, axis=1)
    local_logits = jnp.dot(scaled, router_weight, precision=lax.Precision.HIGHEST)
    squares, logits_raw = lax.psum((local_squares, local_logits), "units")
    inv_rms = lax.rsqrt(squares / D + eps)
    logits = logits_raw * inv_rms[:, None]
    normed = (scaled * inv_rms[:, None]).astype(jnp.bfloat16)
    expert_range = jnp.arange(EXPERTS, dtype=jnp.int32)
    picked = (expert_ids[:, :, None] == expert_range[None, None, :]).astype(jnp.float32)
    chosen = jnp.sum(logits[:, None, :] * picked, axis=-1)
    gates = jax.nn.softmax(chosen, axis=1)
    per_expert = lax.axis_size("units") // EXPERTS
    expert_here = lax.axis_index("units") // per_expert
    weight_row = jnp.sum(gates * (expert_ids == expert_here).astype(jnp.float32), axis=1)
    rows_in = lax.all_gather(normed, "units", axis=1, tiled=True)
    expert_out = expert_block(rows_in, gate_weight, up_weight, down_weight)
    contribution = weight_row[:, None] * expert_out
    spread = lax.psum_scatter(
        contribution.astype(jnp.bfloat16), "units", scatter_dimension=1, tiled=True
    )
    mixture = lax.psum(spread, "cuts").astype(jnp.float32)
    return (hidden_state + mixture).astype(jnp.bfloat16)


def solution(mesh):
    placed = (
        P("groups", "units"),
        P(("groups", "units"), "cuts"),
        P(("groups", "units"), None, "cuts"),
        P(("groups", "units"), None, "cuts"),
        P(("groups", "units"), "cuts"),
        P(("groups", "units"), "cuts"),
        P(("groups", "units")),
        P("cuts", "units"),
        P("units", None),
        P("units"),
        P("groups", None),
        P(None, ("units", "cuts")),
        P(None, ("units", "cuts")),
        P(("units", "cuts"), None),
    )
    return jax.shard_map(
        shards, mesh=mesh, in_specs=placed, out_specs=P("groups", "units"), check_vma=False
    )
```

profile of v0, /device:TPU:0, one launch (start us, length us, event | category | flops | bytes accessed | tf_op | source)
XLA Modules:
  0.0 206.6 jit_solution(990964732860490754)
XLA Ops:
  6.5 0.0 copy-start
  6.5 0.0 all-reduce.4.cloned.1.call-start
  6.5 0.7 iota_compare_fusion
  7.3 0.7 reshape.57
  8.0 0.7 reshape.53
  8.7 1.0 reshape.49
  9.8 0.0 copy-start.7
  9.8 0.2 fusion.38
  10.0 5.9 %fusion.37 = (f32[16,4,6]{2,1,0:T(4,128)S(1)}, f32[16,4,6,512]{3,2,1,0:T(8,128)S(1)}) fusion(bf16[16,4,6,128]{3,2,1,0:T(8,128)(2,1)S(1)} %reshape.49, pred[16,512]{1,0:T(8,128)(4,1)S(1)} %iota_compare_fusion, bf16[16,512,512]{2,1,0:T(8,128)(2,1)} %param.16), kind=kOutput, calls=%fused_computation.47 | convolution fusion | flops 50921088 | bytes 9283072 | tf_op jit(solution)/shard_map/rkgd,rtkd->rkgt/dot_general | solution.py:26
  15.9 0.4 fusion.25
  16.3 0.0 copy-done.7
  16.3 0.0 copy-start.4
  16.4 0.0 copy-start.5
  16.4 0.0 copy-start.6
  16.4 1.3 fusion.17
  17.7 0.1 convert_element_type.52
  17.9 17.2 %all_gather.6 = bf16[128,3072]{1,0:T(8,128)(2,1)S(1)} all-gather(bf16[16,3072]{1,0:T(8,128)(2,1)S(1)} %convert_element_type.52), channel_id=1, replica_groups=mesh['groups'=2,'units'=8,'cuts'=2] {'units'}, dimensions={0}, use_global_device_ids=true | all-gather | bytes 884736 | tf_op jit(solution)/shard_map/all_gather | solution.py:74
  35.1 3.9 %fusion.39 = f32[128,768]{1,0:T(8,128)} fusion(bf16[128,3072]{1,0:T(8,128)(2,1)S(1)} %all_gather.6, bf16[3072,768]{1,0:T(8,128)(2,1)} %param.21), kind=kOutput, calls=%fused_computation.49 | convolution fusion | flops 603979776 | bytes 5898240 | tf_op jit(solution)/shard_map/dot_general | solution.py:73
  39.0 0.0 all-reduce.4.cloned.1.call-update
  39.0 0.0 all-gather.2.cloned.1.call-start
  39.0 27.0 %all-reduce.4.cloned.1.call-done = f32[128,768]{1,0:T(8,128)} async-done(((f32[128,768]{1,0:T(8,128)}), f32[128,768]{1,0:T(8,128)}) %all-reduce.4.cloned.1.call-update) | async-done | bytes 393232 | tf_op jit(solution)/shard_map/psum | solution.py:78
  66.1 0.0 copy-done.4
  66.1 1.1 multiply_reduce_fusion
  67.2 0.0 copy-done
  67.2 0.0 copy-done.5
  67.2 1.4 fusion.29
  68.7 16.4 %all-reduce = (f32[128]{0:T(128)S(1)}, f32[128,4]{0,1:T(4,128)S(1)}) all-reduce(f32[128]{0:T(128)S(1)} %multiply_reduce_fusion, f32[128,4]{0,1:T(4,128)S(1)} %fusion.29), channel_id=1, replica_groups=mesh['groups'=2,'units'=8,'cuts'=2] {'units'}, use_global_device_ids=true, to_apply=%region_5.6 | all-reduce | flops 640 | bytes 5120 | tf_op jit(solution)/shard_map/psum | solution.py:83
  85.0 1.8 multiply_convert_fusion
  86.8 0.0 all-gather.2.cloned.1.call-update
  86.8 0.0 reduce-scatter.2.cloned.1.call-start
  86.9 0.0 copy-done.6
  87.0 22.3 %all-gather.2.cloned.1.call-done = bf16[128,6144]{1,0:T(8,128)(2,1)} async-done(((bf16[128,768]{1,0:T(8,128)(2,1)}), bf16[128,6144]{1,0:T(8,128)(2,1)}) %all-gather.2.cloned.1.call-update) | async-done | bytes 1572880 | tf_op jit(solution)/shard_map/all_gather | solution.py:94
  109.3 0.0 copy-start.2
  109.3 12.0 %fusion.40 = f32[128,2048]{1,0:T(8,128)S(1)} fusion(bf16[128,6144]{1,0:T(8,128)(2,1)} %all-gather.2.cloned.1.call-done, bf16[6144,2048]{1,0:T(8,128)(2,1)} %param.25), kind=kOutput, calls=%fused_computation.50 | convolution fusion | flops 3221225472 | bytes 27787264 | tf_op jit(solution)/shard_map/dot_general | solution.py:50
  121.3 0.0 copy-done.2
  121.3 0.0 copy-start.3
  121.3 0.0 copy-start.1
  121.3 20.5 %fusion.6 = bf16[128,6144]{1,0:T(8,128)(2,1)} fusion(bf16[2048,6144]{1,0:T(8,128)(2,1)} %param.27, bf16[128,6144]{1,0:T(8,128)(2,1)S(1)} %copy-done.2, bf16[6144,2048]{1,0:T(8,128)(2,1)} %param.26, f32[128]{0:T(128)S(1)} %fusion.34, f32[128,2048]{1,0:T(8,128)S(1)} %fusion.40), kind=kOutput, calls=%fused_computation.7 | convolution fusion | flops 6445596672 | bytes 54526464 | tf_op jit(solution)/shard_map/dot_general | solution.py:53
  141.8 0.0 reduce-scatter.2.cloned.1.call-update
  141.9 0.0 all-reduce.6.cloned.1.call-start
  141.9 33.9 %reduce-scatter.2.cloned.1.call-done = bf16[128,768]{1,0:T(8,128)(2,1)} async-done(((bf16[128,6144]{1,0:T(8,128)(2,1)}), bf16[128,768]{1,0:T(8,128)(2,1)}) %reduce-scatter.2.cloned.1.call-update) | async-done | bytes 196624 | tf_op jit(solution)/shard_map/reduce_scatter | solution.py:97
  175.8 0.0 all-reduce.6.cloned.1.call-update
  175.8 22.6 %all-reduce.6.cloned.1.call-done = bf16[128,768]{1,0:T(8,128)(2,1)} async-done(((bf16[128,768]{1,0:T(8,128)(2,1)}), bf16[128,768]{1,0:T(8,128)(2,1)}) %all-reduce.6.cloned.1.call-update) | async-done | bytes 196624 | tf_op jit(solution)/shard_map/psum | solution.py:100
  198.4 0.0 copy-done.3
  198.4 1.7 add_convert_fusion
  200.1 0.0 copy-done.1
  (8 shorter events, 0.2 us)
Async XLA Ops:
  6.5 60.7 %copy-start = (f32[768,4]{0,1:T(4,128)S(1)}, f32[768,4]{0,1:T(4,128)}, u32[]{:S(2)}) copy-start(f32[768,4]{0,1:T(4,128)} %param.22) | copy-start | bytes 36868
  6.5 59.6 %all-reduce.4.cloned.1.call-start = ((), (), s32[]{:S(2)}) async-start(), calls=%async_computation.1 | async-start | bytes 786432 | tf_op jit(solution)/shard_map/psum | solution.py:78
  9.8 6.6 %copy-start.7 = (bf16[16,512,512]{2,1,0:T(8,128)(2,1)S(1)}, bf16[16,512,512]{2,1,0:T(8,128)(2,1)}, u32[]{:S(2)}) copy-start(bf16[16,512,512]{2,1,0:T(8,128)(2,1)} %param.17) | copy-start | bytes 25165828
  16.3 49.7 %copy-start.4 = (bf16[128,768]{1,0:T(8,128)(2,1)S(1)}, bf16[128,768]{1,0:T(8,128)(2,1)}, u32[]{:S(2)}) copy-start(bf16[128,768]{1,0:T(8,128)(2,1)} %param.14) | copy-start | bytes 589828
  16.4 50.9 %copy-start.5 = (f32[768]{0:T(1024)S(1)}, f32[768]{0:T(1024)}, u32[]{:S(2)}) copy-start(f32[768]{0:T(1024)} %param.23) | copy-start | bytes 9220
  16.4 70.5 %copy-start.6 = (s32[128,2]{0,1:T(2,128)S(1)}, s32[128,2]{0,1:T(2,128)}, u32[]{:S(2)}) copy-start(s32[128,2]{0,1:T(2,128)} %param.24) | copy-start | bytes 3076
  39.0 70.3 %all-gather.2.cloned.1.call-start = ((), (), s32[]{:S(2)}) async-start(), calls=%async_computation.2 | async-start | bytes 1769472 | tf_op jit(solution)/shard_map/all_gather | solution.py:94
  86.8 89.0 %reduce-scatter.2.cloned.1.call-start = ((), (), s32[]{:S(2)}) async-start(), calls=%async_computation.3 | async-start | bytes 1769472 | tf_op jit(solution)/shard_map/reduce_scatter | solution.py:97
  109.3 12.0 %copy-start.2 = (bf16[128,6144]{1,0:T(8,128)(2,1)S(1)}, bf16[128,6144]{1,0:T(8,128)(2,1)}, u32[]{:S(2)}) copy-start(bf16[128,6144]{1,0:T(8,128)(2,1)} %all-gather.2.cloned.1.call-done) | copy-start | bytes 4718596
  121.3 77.1 %copy-start.3 = (f32[128,768]{1,0:T(8,128)S(1)}, f32[128,768]{1,0:T(8,128)}, u32[]{:S(2)}) copy-start(f32[128,768]{1,0:T(8,128)} %all-reduce.4.cloned.1.call-done) | copy-start | bytes 1179652
  121.3 78.8 %copy-start.1 = (f32[768,4]{0,1:T(4,128)S(1)}, f32[768,4]{0,1:T(4,128)}, u32[]{:S(2)}) copy-start(f32[768,4]{0,1:T(4,128)} %param.22) | copy-start | bytes 36868
  141.9 56.6 %all-reduce.6.cloned.1.call-start = ((), (), s32[]{:S(2)}) async-start(), calls=%async_computation.4 | async-start | bytes 393216 | tf_op jit(solution)/shard_map/psum | solution.py:100
Sparse Core Ops, SparseCore 0:
  39.1 26.9 all-reduce.3
  86.9 22.2 all-gather.1
  142.0 33.7 reduce-scatter.1
  178.0 20.3 all-reduce.5
where the time goes:
time: 207 us
  waiting for transfers between devices  106 us (51%)
  matrix products  45.2 us (22%)
  blocking collectives  33.6 us (16%)
  between operations  13.3 us (6%)
  other arithmetic  5.85 us (3%)
  local copies, waits for them, and re-layouts  2.68 us (1%)
    reduce_scatter x1, waiting for transfers between devices, shards(): lax.psum_scatter(contribution.astype(jnp.bfloat16), 'units', scatter_dime...  33.9 us
    psum x1, waiting for transfers between devices, shards(): projected = lax.psum(partial_out, 'cuts')  27 us
    psum x1, waiting for transfers between devices, shards(): mixture = lax.psum(spread, 'cuts').astype(jnp.float32)  22.6 us
    all_gather x1, waiting for transfers between devices, shards(): rows_in = lax.all_gather(normed, 'units', axis=1, tiled=True)  22.3 us
    dot_general x1, matrix products, expert_block(): return jnp.dot(inner, down_weight, preferred_element_type=jnp.float32)  20.5 us
    all_gather x1, blocking collectives, shards(): lax.all_gather(attended, 'units', axis=0, tiled=True)  17.2 us
    psum x1, blocking collectives, shards(): squares, logits_raw = lax.psum((local_squares, local_logits), 'units')  16.4 us
    dot_general x1, matrix products, expert_block(): jnp.dot(rows_in, gate_weight, preferred_element_type=jnp.float32)  12 us
  transfers between devices with their start and end apart: 4, of which 4 were waited for; matrix products, arithmetic and copies ran while one was open for 0% of the time, Pallas kernels for 0%

commit v1 on v0

--- a/solution.py
+++ b/solution.py
@@ -1,6 +1,10 @@
+import functools
+
 import jax
 import jax.numpy as jnp
 from jax import lax
+from jax.experimental import pallas as pl
+from jax.experimental.pallas import tpu as pltpu
 from jax.sharding import PartitionSpec as P
 
 D = 6144
@@ -101,6 +105,381 @@
     return (hidden_state + mixture).astype(jnp.bfloat16)
 
 
+F32 = jnp.float32
+BF16 = jnp.bfloat16
+W_SLOTS = 6
+D_SLOTS = 4
+PLANES = 4
+CORES = 2
+CUTS = 2
+
+
+def partner(z, j):
+    if j == 0:
+        return z
+    if j == 1:
+        return z + 1 - 2 * lax.rem(z, 2)
+    if j == 2:
+        return lax.rem(z + 2, 4)
+    return 3 - z
+
+
+def dot(a, b, dims=((1,), (0,)), precision=None):
+    return lax.dot_general(a, b, (dims, ((), ())), precision=precision, preferred_element_type=F32)
+
+
+def layer_kernel(
+    att, residual, gain, router_t, ids, ids_t, out_w, gate_w, up_w, down_w,
+    out,
+    wo, wg, wu, wd, a, psend, precv, hid, xs, x_in, accg, accu, inner, yf,
+    ycs, ycr, yxs, yxr, yzs, yzr, fin, ssend, srecv,
+    sem_o, sem_g, sem_u, sem_d,
+    gz_s, gz_r, gc_s, gc_r, p_s, p_r, dz_s, dz_r, dx_s, dx_r, dc_s, dc_r,
+    st_s, st_r, yc_s, yc_r, yx_s, yx_r, yz_s, yz_r, f_s, f_r,
+):
+    g, u, x = lax.axis_index("groups"), lax.axis_index("units"), lax.axis_index("cuts")
+    z, c = u // CORES, lax.rem(u, CORES)
+    rows = a.shape[0]
+    row_block = att.shape[0]
+    block = wd.shape[2]
+    half = block // CUTS
+    cap = x_in.shape[0]
+    units = PLANES * CORES
+    count = units * CUTS
+    me = u * CUTS + x
+    ox, oc = 1 - x, 1 - c
+    pending = []
+
+    def unit(plane, core):
+        return plane * CORES + core
+
+    def remote(src, dst, ss, rs, to_unit, to_cut):
+        return pltpu.make_async_remote_copy(
+            src_ref=src, dst_ref=dst, send_sem=ss, recv_sem=rs,
+            device_id=(g, to_unit, to_cut), device_id_type=pl.DeviceIdType.MESH,
+        )
+
+    def send(*args):
+        copy = remote(*args)
+        copy.start()
+        pending.append(copy)
+        return copy
+
+    copy_o = pltpu.make_async_copy(out_w, wo, sem_o)
+    copy_o.start()
+
+    barrier = pltpu.get_barrier_semaphore()
+    for k in range(1, count):
+        t = lax.rem(me + k, count)
+        pl.semaphore_signal(barrier, inc=1, device_id=(g, t // CUTS, lax.rem(t, CUTS)), device_id_type=pl.DeviceIdType.MESH)
+
+    def cols_of(index):
+        return pl.ds(pl.multiple_of(index * block, 128), block)
+
+    chunks = [(j, own) for j in range(PLANES) for own in (True, False)]
+
+    def chunk_unit(k):
+        j, own = chunks[k]
+        return unit(partner(z, j), c if own else oc)
+
+    def weight_copies(k):
+        slot = k % W_SLOTS
+        part = pl.ds(pl.multiple_of(chunk_unit(k) * block, 128), block)
+        return (
+            pltpu.make_async_copy(gate_w.at[part, :], wg.at[slot], sem_g.at[slot]),
+            pltpu.make_async_copy(up_w.at[part, :], wu.at[slot], sem_u.at[slot]),
+        )
+
+    def start_weights(k):
+        for copy in weight_copies(k):
+            copy.start()
+
+    d_chunks = [(j, own) for j in (3, 2, 1, 0) for own in (False, True)]
+
+    def down_copy(k):
+        j, own = d_chunks[k]
+        slot = k % D_SLOTS
+        return pltpu.make_async_copy(down_w.at[:, cols_of(unit(partner(z, j), c if own else oc))], wd.at[slot], sem_d.at[slot])
+
+    def rows_of(index):
+        return pl.ds(pl.multiple_of(index * row_block, 16), row_block)
+
+    a[rows_of(u), :] = att[...]
+    pl.semaphore_wait(barrier, count - 1)
+    mine = a.at[rows_of(u), :]
+    for j in (3, 2, 1):
+        send(mine, mine, gz_s.at[j], gz_r.at[j], unit(partner(z, j), c), x)
+    send(mine, mine, gc_s.at[0], gc_r.at[0], unit(z, oc), x)
+
+    copy_o.wait()
+    for k in range(W_SLOTS):
+        start_weights(k)
+    for k in range(D_SLOTS):
+        down_copy(k).start()
+
+    ids_row = ids_t[...]
+    e_iota = lax.broadcasted_iota(jnp.int32, (8, rows), 0)
+    named_t = (ids_row[0:1, :] == e_iota) | (ids_row[1:2, :] == e_iota)
+    r0 = lax.broadcasted_iota(jnp.int32, (rows, rows), 0)
+    r1 = lax.broadcasted_iota(jnp.int32, (rows, rows), 1)
+    upper = jnp.where(r0 <= r1, 1.0, 0.0)
+    place_t = dot(jnp.where(named_t, 1.0, 0.0), upper)
+    place_t = jnp.where(named_t, place_t, 0.0)
+    s_iota = (lax.broadcasted_iota(jnp.int32, (cap, rows), 0) + 1).astype(F32)
+
+    def pick(row):
+        return jnp.where(row == s_iota, 1.0, 0.0)
+
+    for j in (1, 2, 3):
+        there = unit(partner(z, j), c)
+        got = a.at[rows_of(there), :]
+        remote(got, got, gz_s.at[j], gz_r.at[j], there, x).wait_recv()
+        send(got, got, gc_s.at[j], gc_r.at[j], unit(z, oc), x)
+    for j in range(PLANES):
+        got = a.at[rows_of(unit(partner(z, j), oc)), :]
+        remote(got, got, gc_s.at[j], gc_r.at[j], unit(z, oc), x).wait_recv()
+
+    def half_of(index):
+        return pl.ds(pl.multiple_of(index * half, 128), half)
+
+    psend[...] = dot(a[...], wo[:, half_of(ox)]).astype(BF16)
+    psum_copy = send(psend, precv, p_s, p_r, u, ox)
+    own_part = dot(a[...], wo[:, half_of(x)])
+    own_part = own_part + residual[:, half_of(x)].astype(F32)
+    psum_copy.wait_recv()
+    hidden = own_part + precv[...].astype(F32)
+    hid[...] = hidden
+    scaled = hidden * gain[:, half_of(x)]
+    scaled16 = scaled.astype(BF16)
+
+    def line_cols(plane, core, cut):
+        return pl.ds(pl.multiple_of(unit(plane, core) * block + cut * half, 128), half)
+
+    def place_row(expert):
+        return jnp.sum(jnp.where(e_iota == expert, place_t, 0.0), axis=0, keepdims=True)
+
+    for j in (3, 2, 1):
+        to = partner(z, j)
+        xs[j] = dot(pick(place_row(to)).astype(BF16), scaled16).astype(BF16)
+        send(xs.at[j], x_in.at[:, line_cols(z, c, x)], dz_s.at[j], dz_r.at[j], unit(to, c), x)
+    my_pick = pick(place_row(z))
+    x_in[:, line_cols(z, c, x)] = dot(my_pick.astype(BF16), scaled16).astype(BF16)
+
+    def spread(j):
+        plane = partner(z, j)
+        got = x_in.at[:, line_cols(plane, c, x)]
+        if j:
+            remote(got, got, dz_s.at[j], dz_r.at[j], unit(plane, c), x).wait_recv()
+        send(got, got, dx_s.at[j], dx_r.at[j], u, ox)
+        send(got, got, dc_s.at[2 * j], dc_r.at[2 * j], unit(z, oc), x)
+
+    def relay(j):
+        got = x_in.at[:, line_cols(partner(z, j), c, ox)]
+        remote(got, got, dx_s.at[j], dx_r.at[j], u, ox).wait_recv()
+        send(got, got, dc_s.at[2 * j + 1], dc_r.at[2 * j + 1], unit(z, oc), x)
+
+    spread(0)
+    high = lax.Precision.HIGHEST
+    sq = dot(jnp.ones((8, half), F32), hidden * hidden, ((1,), (1,)), high)
+    lg = dot(router_t[:, half_of(x)], scaled, ((1,), (1,)), high)
+    stat = jnp.where(e_iota == 4, sq, lg)
+    ssend[...] = stat
+    for k in range(1, count):
+        t = lax.rem(me + k, count)
+        send(ssend, srecv.at[me], st_s.at[k], st_r.at[me], t // CUTS, lax.rem(t, CUTS))
+
+    def feed(k):
+        j, own = chunks[k]
+        if not own:
+            for i in (0, 1):
+                got = x_in.at[:, line_cols(partner(z, j), oc, x if i == 0 else ox)]
+                remote(got, got, dc_s.at[2 * j + i], dc_r.at[2 * j + i], unit(z, oc), x).wait_recv()
+        for copy in weight_copies(k):
+            copy.wait()
+        slot = k % W_SLOTS
+        tile = 512
+
+        @pl.loop(0, wg.shape[2] // tile)
+        def _(i):
+            cols = pl.ds(pl.multiple_of(i * tile, 128), tile)
+            rows_x = x_in[:, cols_of(chunk_unit(k))]
+            part_g = dot(rows_x, wg[slot, :, cols])
+            part_u = dot(rows_x, wu[slot, :, cols])
+            if k == 0:
+                accg[:, cols] = part_g
+                accu[:, cols] = part_u
+            else:
+                accg[:, cols] += part_g
+                accu[:, cols] += part_u
+
+        if k + W_SLOTS < len(chunks):
+            start_weights(k + W_SLOTS)
+
+    spread(1)
+    relay(0)
+    feed(0)
+    spread(2)
+    relay(1)
+    feed(1)
+    spread(3)
+    relay(2)
+    feed(2)
+    relay(3)
+    for k in range(3, len(chunks)):
+        feed(k)
+
+    total = stat
+    for k in range(1, count):
+        t = lax.rem(me + k, count)
+        remote(ssend, srecv.at[t], st_s.at[k], st_r.at[t], t // CUTS, lax.rem(t, CUTS)).wait_recv()
+        total = total + srecv[t]
+    inv = lax.rsqrt(jnp.sum(jnp.where(e_iota == 4, total, 0.0), axis=0, keepdims=True) / D + eps)
+    inv_col = jnp.sum(my_pick * inv, axis=1, keepdims=True)
+    tile = 512
+
+    @pl.loop(0, inner.shape[1] // tile)
+    def _(i):
+        cols = pl.ds(pl.multiple_of(i * tile, 128), tile)
+        gate_part = accg[:, cols] * inv_col
+        up_part = accu[:, cols] * inv_col
+        inner[:, cols] = (gate_part * jax.nn.sigmoid(gate_part) * up_part).astype(BF16)
+
+    def down_part(k):
+        down_copy(k).wait()
+        slot = k % D_SLOTS
+        tile = 256
+
+        @pl.loop(0, block // tile)
+        def _(i):
+            cols = pl.ds(pl.multiple_of(i * tile, 128), tile)
+            yf[:, cols] = dot(inner[...], wd[slot, :, cols])
+
+        if k + D_SLOTS < len(d_chunks):
+            down_copy(k + D_SLOTS).start()
+
+    def finish(j):
+        remote(yxs.at[j], yxr.at[j], yx_s.at[j], yx_r.at[j], u, ox).wait_recv()
+        yzs[j] = (hid_y[j] + yxr[j].astype(F32)).astype(BF16)
+        if j:
+            send(yzs.at[j], yzr.at[j], yz_s.at[j], yz_r.at[j], unit(partner(z, j), c), x)
+
+    hid_y = {}
+    order = (3, 2, 1, 0)
+    for n, j in enumerate(order):
+        down_part(2 * n)
+        ycs[j] = yf[...].astype(BF16)
+        core_copy = send(ycs.at[j], ycr.at[j], yc_s.at[j], yc_r.at[j], unit(z, oc), x)
+        down_part(2 * n + 1)
+        if n:
+            finish(order[n - 1])
+        core_copy.wait_recv()
+        yf[...] = yf[...] + ycr[j].astype(F32)
+        yxs[j] = yf[:, half_of(ox)].astype(BF16)
+        send(yxs.at[j], yxr.at[j], yx_s.at[j], yx_r.at[j], u, ox)
+        hid_y[j] = yf[:, half_of(x)]
+
+    lane = lax.broadcasted_iota(jnp.int32, (rows, rows), 1)
+    ids_col = ids[...]
+    named = (ids_col[:, 0:1] == lane) | (ids_col[:, 1:2] == lane)
+    lower = jnp.where(r1 <= r0, 1.0, 0.0)
+    place = jnp.where(named, dot(lower, jnp.where(named, 1.0, 0.0)), 0.0)
+    logits = total * inv
+    top = jnp.max(jnp.where(named_t, logits, -jnp.inf), axis=0, keepdims=True)
+    raised = jnp.where(named_t, jnp.exp(jnp.where(named_t, logits - top, 0.0)), 0.0)
+    gates = raised / jnp.sum(raised, axis=0, keepdims=True)
+    spot = (lax.broadcasted_iota(jnp.int32, (rows, cap), 1) + 1).astype(F32)
+
+    def share_of(expert, contribution):
+        weight = jnp.sum(jnp.where(r0 == r1, jnp.sum(jnp.where(e_iota == expert, gates, 0.0), axis=0, keepdims=True), 0.0), axis=1, keepdims=True)
+        column = jnp.sum(jnp.where(lane == expert, place, 0.0), axis=1, keepdims=True)
+        return weight * dot(jnp.where(column == spot, 1.0, 0.0).astype(BF16), contribution)
+
+    mixed = hid[...]
+    for j in (1, 2, 3):
+        if j == 3:
+            finish(0)
+            mixed = mixed + share_of(z, yzs[0])
+        plane = partner(z, j)
+        remote(yzs.at[j], yzr.at[j], yz_s.at[j], yz_r.at[j], unit(plane, c), x).wait_recv()
+        mixed = mixed + share_of(plane, yzr[j])
+    done = mixed.astype(BF16)
+    fin[0] = done
+    last = send(fin.at[0], fin.at[1], f_s, f_r, u, ox)
+    out[:, half_of(x)] = done
+    last.wait_recv()
+    out[:, half_of(ox)] = fin[1]
+    for copy in pending:
+        copy.wait_send()
+
+
+def layer(att, residual, gain, router_t, ids, ids_t, out_w, gate_w, up_w, down_w):
+    rows = residual.shape[0]
+    block = residual.shape[1]
+    half = block // CUTS
+    cap = rows * 5 // 8
+    hidden_units = gate_w.shape[1]
+    count = PLANES * CORES * CUTS
+    vmem = pl.BlockSpec(memory_space=pltpu.VMEM)
+    hbm = pl.BlockSpec(memory_space=pl.ANY)
+    dma = pltpu.SemaphoreType.DMA
+    return pl.pallas_call(
+        layer_kernel,
+        out_shape=jax.ShapeDtypeStruct((rows, block), BF16),
+        in_specs=[vmem] * 6 + [hbm] * 4,
+        out_specs=vmem,
+        scratch_shapes=[
+            pltpu.VMEM(out_w.shape, BF16),
+            pltpu.VMEM((W_SLOTS, block, hidden_units), BF16),
+            pltpu.VMEM((W_SLOTS, block, hidden_units), BF16),
+            pltpu.VMEM((D_SLOTS, hidden_units, block), BF16),
+            pltpu.VMEM((rows, att.shape[1]), BF16),
+            pltpu.VMEM((rows, half), BF16),
+            pltpu.VMEM((rows, half), BF16),
+            pltpu.VMEM((rows, half), F32),
+            pltpu.VMEM((PLANES, cap, half), BF16),
+            pltpu.VMEM((cap, D), BF16),
+            pltpu.VMEM((cap, hidden_units), F32),
+            pltpu.VMEM((cap, hidden_units), F32),
+            pltpu.VMEM((cap, hidden_units), BF16),
+            pltpu.VMEM((cap, block), F32),
+            pltpu.VMEM((PLANES, cap, block), BF16),
+            pltpu.VMEM((PLANES, cap, block), BF16),
+            pltpu.VMEM((PLANES, cap, half), BF16),
+            pltpu.VMEM((PLANES, cap, half), BF16),
+            pltpu.VMEM((PLANES, cap, half), BF16),
+            pltpu.VMEM((PLANES, cap, half), BF16),
+            pltpu.VMEM((2, rows, half), BF16),
+            pltpu.VMEM((8, rows), F32),
+            pltpu.VMEM((count, 8, rows), F32),
+            dma(()), dma((W_SLOTS,)), dma((W_SLOTS,)), dma((D_SLOTS,)),
+            dma((4,)), dma((4,)), dma((4,)), dma((4,)), dma(()), dma(()),
+            dma((4,)), dma((4,)), dma((4,)), dma((4,)), dma((8,)), dma((8,)),
+            dma((count,)), dma((count,)),
+            dma((4,)), dma((4,)), dma((4,)), dma((4,)), dma((4,)), dma((4,)),
+            dma(()), dma(()),
+        ],
+        compiler_params=pltpu.CompilerParams(
+            collective_id=0, has_side_effects=True, vmem_limit_bytes=VMEM_MIB * 2**20
+        ),
+        name="layer",
+    )(att, residual, gain, router_t, ids, ids_t, out_w, gate_w, up_w, down_w)
+
+
+VMEM_MIB = 62
+
+
+def fused_shards(
+    residual, query, key_cache, value_cache, new_key, new_value, lengths, out_weight,
+    router_weight, norm_gain, expert_ids, gate_weight, up_weight, down_weight,
+):
+    attended = attend(query, key_cache, value_cache, new_key, new_value, lengths)
+    router_t = jnp.pad(router_weight.T, ((0, 8 - EXPERTS), (0, 0)))
+    return layer(
+        attended, residual, norm_gain[None, :], router_t, expert_ids, expert_ids.T,
+        out_weight, gate_weight, up_weight, down_weight,
+    )
+
+
 def solution(mesh):
     placed = (
         P("groups", "units"),
@@ -118,6 +497,7 @@
         P(None, ("units", "cuts")),
         P(("units", "cuts"), None),
     )
+    fits = (mesh.shape["units"], mesh.shape["cuts"]) == (PLANES * CORES, CUTS)
     return jax.shard_map(
-        shards, mesh=mesh, in_specs=placed, out_specs=P("groups", "units"), check_vma=False
-    )
+        fused_shards if fits else shards, mesh=mesh, in_specs=placed, out_specs=P("groups", "units"), check_vma=False
+    )

time: 207 us -> 85.2 us (0.41)
  waiting for transfers between devices: 106 us -> 0 us
  Pallas kernels: 0 us -> 67.5 us
  matrix products: 45.2 us -> 10.7 us
  blocking collectives: 33.6 us -> 0 us
  between operations: 13.3 us -> 0.09 us
  other arithmetic: 5.85 us -> 1.16 us
  local copies, waits for them, and re-layouts: 2.68 us -> 5.44 us
    pallas_call x0 -> x1, Pallas kernels: none -> 67.5 us  [layer(): pl.pallas_call(layer_kernel, out_shape=jax.ShapeDtypeStruct((rows, block)...]
    psum x2 -> x0, waiting for transfers between devices: 49.6 us -> none  [the longest x1 27 us: shards(): projected = lax.psum(partial_out, 'cuts')]
    dot_general x4 -> x0, matrix products: 37.8 us -> none  [the longest x1 20.5 us: expert_block(): return jnp.dot(inner, down_weight, preferred_element_type=jnp.float32)]
    reduce_scatter x1 -> x0, waiting for transfers between devices: 33.9 us -> none  [shards(): lax.psum_scatter(contribution.astype(jnp.bfloat16), 'units', scatter_dime...]
    all_gather x1 -> x0, waiting for transfers between devices: 22.3 us -> none  [shards(): rows_in = lax.all_gather(normed, 'units', axis=1, tiled=True)]
    all_gather x1 -> x0, blocking collectives: 17.2 us -> none  [shards(): lax.all_gather(attended, 'units', axis=0, tiled=True)]
    psum x1 -> x0, blocking collectives: 16.4 us -> none  [shards(): squares, logits_raw = lax.psum((local_squares, local_logits), 'units')]
    convert_element_type x2 -> x0, other arithmetic: 3.45 us -> none  [the longest x1 1.77 us: shards(): normed = (scaled * inv_rms[:, None]).astype(jnp.bfloat16)]
  transfers between devices with their start and end apart: 4 -> 0, of which waited for: 4 -> 0; matrix products, arithmetic and copies ran while one was open for 0% -> 0% of each run, Pallas kernels for 0% -> 0%
where the time goes in v1:
time: 85.2 us; the launch traced here: 84.9 us
  Pallas kernels  67.5 us (79%)
  matrix products  10.7 us (13%)
  local copies, waits for them, and re-layouts  5.44 us (6%)
  other arithmetic  1.16 us (1%)
    pallas_call x1, Pallas kernels, layer(): pl.pallas_call(layer_kernel, out_shape=jax.ShapeDtypeStruct((rows, block)...  67.5 us
    dot_general x1, matrix products, attend(): jnp.einsum('rkgd,rtkd->rkgt', q_heads, keys_all, preferred_element_type=j...  5.74 us
    dot_general x1, matrix products, attend(): jnp.einsum('rkgt,rtkd->rkgd', probs, values_all, preferred_element_type=j...  4.76 us
    unnamed x12, local copies, waits for them, and re-layouts  2.38 us

profile of v1, /device:TPU:0, one launch (start us, length us, event | category | flops | bytes accessed | tf_op | source)
XLA Modules:
  0.0 84.9 jit_solution(9308663746893625254)
XLA Ops:
  0.0 0.0 copy-start
  0.0 0.0 copy-start.1
  0.0 1.0 %reshape.42 = bf16[16,4,6,128]{3,2,1,0:T(8,128)(2,1)S(1)} reshape(bf16[16,3072]{1,0:T(8,128)(2,1)} %param.15) | data formatting | bytes 196608 | tf_op jit(solution)/shard_map/reshape | solution.py:24
  1.1 0.7 iota_compare_fusion
  1.8 5.7 %fusion.23 = (f32[16,4,6]{2,1,0:T(4,128)S(1)}, f32[16,4,6,512]{3,2,1,0:T(8,128)S(1)}) fusion(bf16[16,4,6,128]{3,2,1,0:T(8,128)(2,1)S(1)} %reshape.42, pred[16,512]{1,0:T(8,128)(4,1)S(1)} %iota_compare_fusion, bf16[16,512,512]{2,1,0:T(8,128)(2,1)} %param.16), kind=kOutput, calls=%fused_computation.21 | convolution fusion | flops 50921088 | bytes 9283072 | tf_op jit(solution)/shard_map/rkgd,rtkd->rkgt/dot_general | solution.py:30
  7.5 0.0 copy-start.4
  7.5 0.0 copy-start.2
  7.6 0.0 copy-start.3
  7.6 0.0 copy-done
  7.6 0.2 fusion.24
  7.8 0.4 fusion.18
  8.2 0.0 copy-done.1
  8.3 4.8 %fusion.15 = bf16[16,4,6,128]{3,2,1,0:T(8,128)(2,1)S(1)} fusion(f32[16,4,6,512]{3,2,1,0:T(8,128)S(1)} %get-tuple-element.8, f32[16,4,6]{2,1,0:T(4,128)S(1)} %get-tuple-element.6, f32[16,4,6]{2,1,0:T(4,128)S(1)} %multiply_maximum_fusion, f32[16,4,128]{2,1,0:T(4,128)S(1)} %reshape.46, f32[16,4,6]{2,1,0:T(4,128)S(1)} %get-tuple-element.5, ...), kind=kOutput, calls=%fused_computation.9 | convolution fusion | flops 51068928 | bytes 9310720 | tf_op jit(solution)/shard_map/rkgt,rtkd->rkgd/dot_general | solution.py:45
  13.0 0.8 convert_element_type.32.att
  13.8 0.0 copy-done.4
  13.8 0.7 copy.20.ids
  14.6 0.0 copy-done.2
  14.6 0.6 pad.4.router_t
  15.2 0.0 copy-done.3
  15.2 0.6 broadcast_in_dim.24.gain
  15.8 67.5 %layer.1 = bf16[128,768]{1,0:T(8,128)(2,1)} custom-call(bf16[16,3072]{1,0:T(8,128)(2,1)} %convert_element_type.32.att, bf16[128,768]{1,0:T(8,128)(2,1)} %residual.1, f32[1,768]{1,0:T(1,128)} %broadcast_in_dim.24.gain, f32[8,768]{1,0:T(8,128)} %pad.4.router_t, s32[128,2]{1,0:T(8,128)} %copy.20.ids, s32[2,128]{1,0:T(2,128)} %bitcast.34, ...), custom_call_target="tpu_custom_call" | custom-call | tf_op jit(solution)/shard_map/layer/pallas_call | solution.py:425
  83.3 1.6 %copy.44 = bf16[128,768]{1,0:T(8,128)(2,1)} copy(bf16[128,768]{1,0:T(8,128)(2,1)} %layer.1) | data formatting | bytes 393216
  (4 shorter events, 0.1 us)
Async XLA Ops:
  0.0 7.6 %copy-start = (bf16[16,512]{1,0:T(8,128)(2,1)S(1)}, bf16[16,512]{1,0:T(8,128)(2,1)}, u32[]{:S(2)}) copy-start(bf16[16,512]{1,0:T(8,128)(2,1)} %param.18) | copy-start | bytes 49156
  0.0 8.2 %copy-start.1 = (bf16[16,512]{1,0:T(8,128)(2,1)S(1)}, bf16[16,512]{1,0:T(8,128)(2,1)}, u32[]{:S(2)}) copy-start(bf16[16,512]{1,0:T(8,128)(2,1)} %param.19) | copy-start | bytes 49156
  7.5 6.3 %copy-start.4 = (s32[128,2]{0,1:T(2,128)S(1)}, s32[128,2]{0,1:T(2,128)}, u32[]{:S(2)}) copy-start(s32[128,2]{0,1:T(2,128)} %param.24) | copy-start | bytes 3076
  7.5 7.0 %copy-start.2 = (f32[768,4]{0,1:T(4,128)S(1)}, f32[768,4]{0,1:T(4,128)}, u32[]{:S(2)}) copy-start(f32[768,4]{0,1:T(4,128)} %param.22) | copy-start | bytes 36868
  7.6 7.6 %copy-start.3 = (f32[768]{0:T(1024)S(1)}, f32[768]{0:T(1024)}, u32[]{:S(2)}) copy-start(f32[768]{0:T(1024)} %param.23) | copy-start | bytes 9220

commit v2 on v1

--- a/solution.py
+++ b/solution.py
@@ -129,18 +129,18 @@
 
 
 def layer_kernel(
-    att, residual, gain, router_t, ids, ids_t, out_w, gate_w, up_w, down_w,
+    query, new_key, new_value, lengths, residual, gain, router_t, ids, ids_t, key_cache, value_cache, out_w, gate_w, up_w, down_w,
     out,
-    wo, wg, wu, wd, a, psend, precv, hid, xs, x_in, accg, accu, inner, yf,
+    wo, wg, wu, wd, qs, os, nk, nv, a, psend, precv, hid, xs, x_in, accg, accu, inner, yf,
     ycs, ycr, yxs, yxr, yzs, yzr, fin, ssend, srecv,
-    sem_o, sem_g, sem_u, sem_d,
+    sem_o, sem_g, sem_u, sem_d, sem_kv,
     gz_s, gz_r, gc_s, gc_r, p_s, p_r, dz_s, dz_r, dx_s, dx_r, dc_s, dc_r,
     st_s, st_r, yc_s, yc_r, yx_s, yx_r, yz_s, yz_r, f_s, f_r,
 ):
     g, u, x = lax.axis_index("groups"), lax.axis_index("units"), lax.axis_index("cuts")
     z, c = u // CORES, lax.rem(u, CORES)
     rows = a.shape[0]
-    row_block = att.shape[0]
+    row_block = query.shape[0]
     block = wd.shape[2]
     half = block // CUTS
     cap = x_in.shape[0]
@@ -165,6 +165,21 @@
         pending.append(copy)
         return copy
 
+    slots, lanes = key_cache.shape[1], key_cache.shape[2]
+    steps = row_block // 2
+
+    def cache_copies(step, slot):
+        for i in range(2):
+            for n, cache in enumerate((key_cache, value_cache)):
+                yield pltpu.make_async_copy(
+                    cache.at[2 * step + i],
+                    wd.at[slot, pl.ds((2 * i + n) * slots, slots), pl.ds(0, lanes)],
+                    sem_kv.at[slot, 2 * i + n],
+                )
+
+    for step in range(D_SLOTS):
+        for copy in cache_copies(step, step):
+            copy.start()
     copy_o = pltpu.make_async_copy(out_w, wo, sem_o)
     copy_o.start()
 
@@ -204,7 +219,60 @@
     def rows_of(index):
         return pl.ds(pl.multiple_of(index * row_block, 16), row_block)
 
-    a[rows_of(u), :] = att[...]
+    heads = query.shape[1] // HD
+    kv_heads = lanes // HD
+    share = heads // kv_heads
+    qs[...] = query[...].astype(F32).reshape(row_block, heads, HD)
+    own_head = (
+        lax.broadcasted_iota(jnp.int32, (heads, lanes), 0) // share
+        == lax.broadcasted_iota(jnp.int32, (heads, lanes), 1) // HD
+    )
+    slot_iota = lax.broadcasted_iota(jnp.int32, (heads, slots), 1)
+
+    def attend_step(step, slot):
+        for copy in cache_copies(step, slot):
+            copy.wait()
+        for i in range(2):
+            row = 2 * step + i
+            q = jnp.where(own_head, jnp.concatenate([qs[row]] * kv_heads, axis=1), 0.0)
+            keys = wd[slot, pl.ds(2 * i * slots, slots), pl.ds(0, lanes)]
+            values = wd[slot, pl.ds((2 * i + 1) * slots, slots), pl.ds(0, lanes)]
+            scores = dot(q.astype(BF16), keys, ((1,), (1,))) * HD ** (-0.5)
+            own = jnp.sum(q * nk[pl.ds(row, 1), :], axis=1, keepdims=True) * HD ** (-0.5)
+            valid = slot_iota < lengths[row]
+            highest = jnp.maximum(jnp.max(jnp.where(valid, scores, -jnp.inf), axis=1, keepdims=True), own)
+            weights = jnp.where(valid, jnp.exp(jnp.where(valid, scores - highest, 0.0)), 0.0)
+            own_weight = jnp.exp(own - highest)
+            all_weight = jnp.sum(weights, axis=1, keepdims=True) + own_weight
+            probs = (weights / all_weight).astype(BF16)
+            own_prob = (own_weight / all_weight).astype(BF16).astype(F32)
+            mix = dot(probs, values) + own_prob * nv[pl.ds(row, 1), :]
+            mix = jnp.where(own_head, mix, 0.0)
+            heads_out = mix[:, :HD]
+            for n in range(1, kv_heads):
+                heads_out = heads_out + mix[:, n * HD:(n + 1) * HD]
+            os[row] = heads_out
+
+    nk[...] = new_key[...].astype(F32)
+    nv[...] = new_value[...].astype(F32)
+
+    @pl.loop(0, steps - D_SLOTS)
+    def _(step):
+        slot = lax.rem(step, D_SLOTS)
+        attend_step(step, slot)
+        for copy in cache_copies(step + D_SLOTS, slot):
+            copy.start()
+
+    for k in range(W_SLOTS):
+        start_weights(k)
+
+    @pl.loop(steps - D_SLOTS, steps)
+    def _(step):
+        attend_step(step, lax.rem(step, D_SLOTS))
+
+    for k in range(D_SLOTS):
+        down_copy(k).start()
+    a[rows_of(u), :] = os[...].reshape(row_block, heads * HD).astype(BF16)
     pl.semaphore_wait(barrier, count - 1)
     mine = a.at[rows_of(u), :]
     for j in (3, 2, 1):
@@ -212,10 +280,6 @@
     send(mine, mine, gc_s.at[0], gc_r.at[0], unit(z, oc), x)
 
     copy_o.wait()
-    for k in range(W_SLOTS):
-        start_weights(k)
-    for k in range(D_SLOTS):
-        down_copy(k).start()
 
     ids_row = ids_t[...]
     e_iota = lax.broadcasted_iota(jnp.int32, (8, rows), 0)
@@ -412,7 +476,7 @@
         copy.wait_send()
 
 
-def layer(att, residual, gain, router_t, ids, ids_t, out_w, gate_w, up_w, down_w):
+def layer(query, new_key, new_value, lengths, residual, gain, router_t, ids, ids_t, key_cache, value_cache, out_w, gate_w, up_w, down_w):
     rows = residual.shape[0]
     block = residual.shape[1]
     half = block // CUTS
@@ -425,14 +489,18 @@
     return pl.pallas_call(
         layer_kernel,
         out_shape=jax.ShapeDtypeStruct((rows, block), BF16),
-        in_specs=[vmem] * 6 + [hbm] * 4,
+        in_specs=[vmem] * 3 + [pl.BlockSpec(memory_space=pltpu.SMEM)] + [vmem] * 5 + [hbm] * 6,
         out_specs=vmem,
         scratch_shapes=[
             pltpu.VMEM(out_w.shape, BF16),
             pltpu.VMEM((W_SLOTS, block, hidden_units), BF16),
             pltpu.VMEM((W_SLOTS, block, hidden_units), BF16),
             pltpu.VMEM((D_SLOTS, hidden_units, block), BF16),
-            pltpu.VMEM((rows, att.shape[1]), BF16),
+            pltpu.VMEM((query.shape[0], query.shape[1] // HD, HD), F32),
+            pltpu.VMEM((query.shape[0], query.shape[1] // HD, HD), F32),
+            pltpu.VMEM(new_key.shape, F32),
+            pltpu.VMEM(new_value.shape, F32),
+            pltpu.VMEM((rows, query.shape[1]), BF16),
             pltpu.VMEM((rows, half), BF16),
             pltpu.VMEM((rows, half), BF16),
             pltpu.VMEM((rows, half), F32),
@@ -451,7 +519,7 @@
             pltpu.VMEM((2, rows, half), BF16),
             pltpu.VMEM((8, rows), F32),
             pltpu.VMEM((count, 8, rows), F32),
-            dma(()), dma((W_SLOTS,)), dma((W_SLOTS,)), dma((D_SLOTS,)),
+            dma(()), dma((W_SLOTS,)), dma((W_SLOTS,)), dma((D_SLOTS,)), dma((D_SLOTS, 4)),
             dma((4,)), dma((4,)), dma((4,)), dma((4,)), dma(()), dma(()),
             dma((4,)), dma((4,)), dma((4,)), dma((4,)), dma((8,)), dma((8,)),
             dma((count,)), dma((count,)),
@@ -462,7 +530,7 @@
             collective_id=0, has_side_effects=True, vmem_limit_bytes=VMEM_MIB * 2**20
         ),
         name="layer",
-    )(att, residual, gain, router_t, ids, ids_t, out_w, gate_w, up_w, down_w)
+    )(query, new_key, new_value, lengths, residual, gain, router_t, ids, ids_t, key_cache, value_cache, out_w, gate_w, up_w, down_w)
 
 
 VMEM_MIB = 62
@@ -472,11 +540,10 @@
     residual, query, key_cache, value_cache, new_key, new_value, lengths, out_weight,
     router_weight, norm_gain, expert_ids, gate_weight, up_weight, down_weight,
 ):
-    attended = attend(query, key_cache, value_cache, new_key, new_value, lengths)
     router_t = jnp.pad(router_weight.T, ((0, 8 - EXPERTS), (0, 0)))
     return layer(
-        attended, residual, norm_gain[None, :], router_t, expert_ids, expert_ids.T,
-        out_weight, gate_weight, up_weight, down_weight,
+        query, new_key, new_value, lengths, residual, norm_gain[None, :], router_t, expert_ids, expert_ids.T,
+        key_cache, value_cache, out_weight, gate_weight, up_weight, down_weight,
     )
 
 

time: 85.2 us -> 81.2 us (0.953)
  matrix products: 10.7 us -> 0 us
  Pallas kernels: 67.5 us -> 75.3 us
  other arithmetic: 1.16 us -> 0 us
    dot_general x3 -> x0, matrix products: 10.7 us -> none  [the longest x1 5.74 us: attend(): jnp.einsum('rkgd,rtkd->rkgt', q_heads, keys_all, preferred_element_type=j...]
    pallas_call x1, Pallas kernels: 67.5 us -> 75.3 us  [layer(): pl.pallas_call(layer_kernel, out_shape=jax.ShapeDtypeStruct((rows, block)...]
    reshape x2 -> x0, local copies, waits for them, and re-layouts: 1.06 us -> none  [the longest x1 1.05 us: attend(): q_heads = query.reshape(row_count, kv_local, share, HD)]
    unnamed x12 -> x2, local copies, waits for them, and re-layouts: 2.38 us -> 3.03 us
where the time goes in v2:
time: 81.2 us; the launch traced here: 81 us
  Pallas kernels  75.3 us (93%)
  local copies, waits for them, and re-layouts  5.62 us (7%)
    pallas_call x1, Pallas kernels, layer(): pl.pallas_call(layer_kernel, out_shape=jax.ShapeDtypeStruct((rows, block)...  75.3 us
    unnamed x2, local copies, waits for them, and re-layouts  3.03 us

profile of v2, /device:TPU:0, one launch (start us, length us, event | category | flops | bytes accessed | tf_op | source)
XLA Modules:
  0.0 81.0 jit_solution(15867457266825364806)
XLA Ops:
  0.0 1.3 %broadcast_in_dim.3.gain = f32[1,768]{1,0:T(1,128)} reshape(f32[768]{0:T(1024)} %param.23) | data formatting | bytes 6144 | tf_op jit(solution)/shard_map/broadcast_in_dim | solution.py:545
  1.3 1.3 %pad.4.router_t = f32[8,768]{1,0:T(8,128)} pad(f32[4,768]{1,0:T(4,128)} %bitcast.2, f32[]{:T(128)} %constant.2.clone.1), padding=0_4x0_0 | pad | bytes 36868 | tf_op jit(solution)/shard_map/jit(_pad)/pad | solution.py:543
  2.6 1.4 %copy.15.ids = s32[128,2]{1,0:T(8,128)} copy(s32[128,2]{0,1:T(2,128)} %param.24) | data formatting | bytes 2048 | tf_op args[10]
  4.0 75.3 %layer.1 = bf16[128,768]{1,0:T(8,128)(2,1)} custom-call(bf16[16,3072]{1,0:T(8,128)(2,1)} %query.1, bf16[16,512]{1,0:T(8,128)(2,1)} %new_key.1, bf16[16,512]{1,0:T(8,128)(2,1)} %new_value.1, s32[16]{0:T(128)} %lengths.1, bf16[128,768]{1,0:T(8,128)(2,1)} %residual.1, f32[1,768]{1,0:T(1,128)} %broadcast_in_dim.3.gain, f32[8,768]{1,0:T(8,128)} %pad.4.router_t, ...), custom_call_target="tpu_custom_call" | custom-call | tf_op jit(solution)/shard_map/layer/pallas_call | solution.py:489
  79.3 1.6 %copy.17 = bf16[128,768]{1,0:T(8,128)(2,1)} copy(bf16[128,768]{1,0:T(8,128)(2,1)} %layer.1) | data formatting | bytes 393216

commit v3 on v2

--- a/solution.py
+++ b/solution.py
@@ -129,9 +129,9 @@
 
 
 def layer_kernel(
-    query, new_key, new_value, lengths, residual, gain, router_t, ids, ids_t, key_cache, value_cache, out_w, gate_w, up_w, down_w,
+    query, new_key, new_value, lengths, residual, gain, router_t, ids_t, key_cache, value_cache, out_w, gate_w, up_w, down_w,
     out,
-    wo, wg, wu, wd, qs, os, nk, nv, a, psend, precv, hid, xs, x_in, accg, accu, inner, yf,
+    wo, wg, wu, wd, qs, os, nk, nv, a, psend, precv, hid, xs, x_in, accg, accu, inner,
     ycs, ycr, yxs, yxr, yzs, yzr, fin, ssend, srecv,
     sem_o, sem_g, sem_u, sem_d, sem_kv,
     gz_s, gz_r, gc_s, gc_r, p_s, p_r, dz_s, dz_r, dx_s, dx_r, dc_s, dc_r,
@@ -165,20 +165,22 @@
         pending.append(copy)
         return copy
 
-    slots, lanes = key_cache.shape[1], key_cache.shape[2]
-    steps = row_block // 2
-
-    def cache_copies(step, slot):
-        for i in range(2):
+    slots = key_cache.shape[1]
+    lanes = key_cache.shape[2] // 2
+    per_step = wd.shape[1] // slots
+    steps = row_block // per_step
+
+    def cache_copies(part, step, slot):
+        for i in range(per_step):
             for n, cache in enumerate((key_cache, value_cache)):
                 yield pltpu.make_async_copy(
-                    cache.at[2 * step + i],
-                    wd.at[slot, pl.ds((2 * i + n) * slots, slots), pl.ds(0, lanes)],
+                    cache.at[per_step * step + i, :, pl.ds(part * lanes, lanes)],
+                    wd.at[slot, pl.ds(i * slots, slots), pl.ds(n * lanes, lanes)],
                     sem_kv.at[slot, 2 * i + n],
                 )
 
-    for step in range(D_SLOTS):
-        for copy in cache_copies(step, step):
+    for step in range(steps):
+        for copy in cache_copies(0, step, step):
             copy.start()
     copy_o = pltpu.make_async_copy(out_w, wo, sem_o)
     copy_o.start()
@@ -219,26 +221,31 @@
     def rows_of(index):
         return pl.ds(pl.multiple_of(index * row_block, 16), row_block)
 
-    heads = query.shape[1] // HD
+    heads = query.shape[1] // HD // 2
     kv_heads = lanes // HD
     share = heads // kv_heads
-    qs[...] = query[...].astype(F32).reshape(row_block, heads, HD)
+    width = heads * HD
+    qs[...] = query[...].astype(F32).reshape(row_block, 2 * heads, HD)
     own_head = (
         lax.broadcasted_iota(jnp.int32, (heads, lanes), 0) // share
         == lax.broadcasted_iota(jnp.int32, (heads, lanes), 1) // HD
     )
     slot_iota = lax.broadcasted_iota(jnp.int32, (heads, slots), 1)
-
-    def attend_step(step, slot):
-        for copy in cache_copies(step, slot):
+    nk[...] = new_key[...].astype(F32)
+    nv[...] = new_value[...].astype(F32)
+
+    def attend_step(part, step):
+        for copy in cache_copies(part, step, step):
             copy.wait()
-        for i in range(2):
-            row = 2 * step + i
-            q = jnp.where(own_head, jnp.concatenate([qs[row]] * kv_heads, axis=1), 0.0)
-            keys = wd[slot, pl.ds(2 * i * slots, slots), pl.ds(0, lanes)]
-            values = wd[slot, pl.ds((2 * i + 1) * slots, slots), pl.ds(0, lanes)]
+        for i in range(per_step):
+            row = per_step * step + i
+            here = slice(part * lanes, (part + 1) * lanes)
+            q = qs[row, part * heads:(part + 1) * heads, :]
+            q = jnp.where(own_head, jnp.concatenate([q] * kv_heads, axis=1), 0.0)
+            keys = wd[step, pl.ds(i * slots, slots), pl.ds(0, lanes)]
+            values = wd[step, pl.ds(i * slots, slots), pl.ds(lanes, lanes)]
             scores = dot(q.astype(BF16), keys, ((1,), (1,))) * HD ** (-0.5)
-            own = jnp.sum(q * nk[pl.ds(row, 1), :], axis=1, keepdims=True) * HD ** (-0.5)
+            own = jnp.sum(q * nk[pl.ds(row, 1), here], axis=1, keepdims=True) * HD ** (-0.5)
             valid = slot_iota < lengths[row]
             highest = jnp.maximum(jnp.max(jnp.where(valid, scores, -jnp.inf), axis=1, keepdims=True), own)
             weights = jnp.where(valid, jnp.exp(jnp.where(valid, scores - highest, 0.0)), 0.0)
@@ -246,39 +253,52 @@
             all_weight = jnp.sum(weights, axis=1, keepdims=True) + own_weight
             probs = (weights / all_weight).astype(BF16)
             own_prob = (own_weight / all_weight).astype(BF16).astype(F32)
-            mix = dot(probs, values) + own_prob * nv[pl.ds(row, 1), :]
+            mix = dot(probs, values) + own_prob * nv[pl.ds(row, 1), here]
             mix = jnp.where(own_head, mix, 0.0)
             heads_out = mix[:, :HD]
             for n in range(1, kv_heads):
                 heads_out = heads_out + mix[:, n * HD:(n + 1) * HD]
-            os[row] = heads_out
-
-    nk[...] = new_key[...].astype(F32)
-    nv[...] = new_value[...].astype(F32)
-
-    @pl.loop(0, steps - D_SLOTS)
+            os[part, row] = heads_out
+
+    def part_of(index, part):
+        return a.at[rows_of(index), pl.ds(part * width, width)]
+
+    def spread_rows(part):
+        a[rows_of(u), pl.ds(part * width, width)] = os[part].reshape(row_block, width).astype(BF16)
+        if part == 0:
+            pl.semaphore_wait(barrier, count - 1)
+        mine = part_of(u, part)
+        for j in (3, 2, 1):
+            send(mine, mine, gz_s.at[4 * part + j], gz_r.at[4 * part + j], unit(partner(z, j), c), x)
+        send(mine, mine, gc_s.at[4 * part], gc_r.at[4 * part], unit(z, oc), x)
+
+    def gather_rows(part):
+        for j in (3, 2, 1):
+            there = unit(partner(z, j), c)
+            got = part_of(there, part)
+            remote(got, got, gz_s.at[4 * part + j], gz_r.at[4 * part + j], there, x).wait_recv()
+            send(got, got, gc_s.at[4 * part + j], gc_r.at[4 * part + j], unit(z, oc), x)
+        for j in range(PLANES):
+            got = part_of(unit(partner(z, j), oc), part)
+            remote(got, got, gc_s.at[4 * part + j], gc_r.at[4 * part + j], unit(z, oc), x).wait_recv()
+
+    @pl.loop(0, steps)
     def _(step):
-        slot = lax.rem(step, D_SLOTS)
-        attend_step(step, slot)
-        for copy in cache_copies(step + D_SLOTS, slot):
+        attend_step(0, step)
+        for copy in cache_copies(1, step, step):
             copy.start()
 
     for k in range(W_SLOTS):
         start_weights(k)
-
-    @pl.loop(steps - D_SLOTS, steps)
+    spread_rows(0)
+
+    @pl.loop(0, steps)
     def _(step):
-        attend_step(step, lax.rem(step, D_SLOTS))
-
+        attend_step(1, step)
+
+    spread_rows(1)
     for k in range(D_SLOTS):
         down_copy(k).start()
-    a[rows_of(u), :] = os[...].reshape(row_block, heads * HD).astype(BF16)
-    pl.semaphore_wait(barrier, count - 1)
-    mine = a.at[rows_of(u), :]
-    for j in (3, 2, 1):
-        send(mine, mine, gz_s.at[j], gz_r.at[j], unit(partner(z, j), c), x)
-    send(mine, mine, gc_s.at[0], gc_r.at[0], unit(z, oc), x)
-
     copy_o.wait()
 
     ids_row = ids_t[...]
@@ -294,26 +314,25 @@
     def pick(row):
         return jnp.where(row == s_iota, 1.0, 0.0)
 
-    for j in (1, 2, 3):
-        there = unit(partner(z, j), c)
-        got = a.at[rows_of(there), :]
-        remote(got, got, gz_s.at[j], gz_r.at[j], there, x).wait_recv()
-        send(got, got, gc_s.at[j], gc_r.at[j], unit(z, oc), x)
-    for j in range(PLANES):
-        got = a.at[rows_of(unit(partner(z, j), oc)), :]
-        remote(got, got, gc_s.at[j], gc_r.at[j], unit(z, oc), x).wait_recv()
-
     def half_of(index):
         return pl.ds(pl.multiple_of(index * half, 128), half)
 
-    psend[...] = dot(a[...], wo[:, half_of(ox)]).astype(BF16)
+    def project(part, cut):
+        here = pl.ds(part * width, width)
+        return dot(a[:, here], wo[here, half_of(cut)])
+
+    gather_rows(0)
+    other_part = project(0, ox)
+    hid[...] = project(0, x) + residual[:, half_of(x)].astype(F32)
+    gather_rows(1)
+    psend[...] = (other_part + project(1, ox)).astype(BF16)
     psum_copy = send(psend, precv, p_s, p_r, u, ox)
-    own_part = dot(a[...], wo[:, half_of(x)])
-    own_part = own_part + residual[:, half_of(x)].astype(F32)
+    own_part = hid[...] + project(1, x)
     psum_copy.wait_recv()
     hidden = own_part + precv[...].astype(F32)
     hid[...] = hidden
-    scaled = hidden * gain[:, half_of(x)]
+    all_gain = gain[...].reshape(1, block)
+    scaled = hidden * jnp.where(x == 0, all_gain[:, :half], all_gain[:, half:])
     scaled16 = scaled.astype(BF16)
 
     def line_cols(plane, core, cut):
@@ -322,7 +341,7 @@
     def place_row(expert):
         return jnp.sum(jnp.where(e_iota == expert, place_t, 0.0), axis=0, keepdims=True)
 
-    for j in (3, 2, 1):
+    for j in (1, 2, 3):
         to = partner(z, j)
         xs[j] = dot(pick(place_row(to)).astype(BF16), scaled16).astype(BF16)
         send(xs.at[j], x_in.at[:, line_cols(z, c, x)], dz_s.at[j], dz_r.at[j], unit(to, c), x)
@@ -346,7 +365,7 @@
     high = lax.Precision.HIGHEST
     sq = dot(jnp.ones((8, half), F32), hidden * hidden, ((1,), (1,)), high)
     lg = dot(router_t[:, half_of(x)], scaled, ((1,), (1,)), high)
-    stat = jnp.where(e_iota == 4, sq, lg)
+    stat = jnp.concatenate([lg, sq[EXPERTS:]], axis=0)
     ssend[...] = stat
     for k in range(1, count):
         t = lax.rem(me + k, count)
@@ -408,7 +427,7 @@
         up_part = accu[:, cols] * inv_col
         inner[:, cols] = (gate_part * jax.nn.sigmoid(gate_part) * up_part).astype(BF16)
 
-    def down_part(k):
+    def down_part(k, dst):
         down_copy(k).wait()
         slot = k % D_SLOTS
         tile = 256
@@ -416,37 +435,38 @@
         @pl.loop(0, block // tile)
         def _(i):
             cols = pl.ds(pl.multiple_of(i * tile, 128), tile)
-            yf[:, cols] = dot(inner[...], wd[slot, :, cols])
+            dst[:, cols] = dot(inner[...], wd[slot, :, cols]).astype(dst.dtype)
 
         if k + D_SLOTS < len(d_chunks):
             down_copy(k + D_SLOTS).start()
 
-    def finish(j):
+    order = (3, 2, 1, 0)
+    yf = [acc.at[:, pl.ds(0, block)] for acc in (accg, accu)]
+
+    def core_stage(n):
+        j = order[n]
+        remote(ycs.at[j], ycr.at[j], yc_s.at[j], yc_r.at[j], unit(z, oc), x).wait_recv()
+        yxs[j] = (yf[n % 2][:, half_of(ox)] + ycr[j, :, half_of(ox)].astype(F32)).astype(BF16)
+        send(yxs.at[j], yxr.at[j], yx_s.at[j], yx_r.at[j], u, ox)
+
+    def cut_stage(n):
+        j = order[n]
+        mine = yf[n % 2][:, half_of(x)] + ycr[j, :, half_of(x)].astype(F32)
         remote(yxs.at[j], yxr.at[j], yx_s.at[j], yx_r.at[j], u, ox).wait_recv()
-        yzs[j] = (hid_y[j] + yxr[j].astype(F32)).astype(BF16)
+        yzs[j] = (mine + yxr[j].astype(F32)).astype(BF16)
         if j:
             send(yzs.at[j], yzr.at[j], yz_s.at[j], yz_r.at[j], unit(partner(z, j), c), x)
 
-    hid_y = {}
-    order = (3, 2, 1, 0)
     for n, j in enumerate(order):
-        down_part(2 * n)
-        ycs[j] = yf[...].astype(BF16)
-        core_copy = send(ycs.at[j], ycr.at[j], yc_s.at[j], yc_r.at[j], unit(z, oc), x)
-        down_part(2 * n + 1)
+        down_part(2 * n, ycs.at[j])
+        send(ycs.at[j], ycr.at[j], yc_s.at[j], yc_r.at[j], unit(z, oc), x)
         if n:
-            finish(order[n - 1])
-        core_copy.wait_recv()
-        yf[...] = yf[...] + ycr[j].astype(F32)
-        yxs[j] = yf[:, half_of(ox)].astype(BF16)
-        send(yxs.at[j], yxr.at[j], yx_s.at[j], yx_r.at[j], u, ox)
-        hid_y[j] = yf[:, half_of(x)]
-
-    lane = lax.broadcasted_iota(jnp.int32, (rows, rows), 1)
-    ids_col = ids[...]
-    named = (ids_col[:, 0:1] == lane) | (ids_col[:, 1:2] == lane)
-    lower = jnp.where(r1 <= r0, 1.0, 0.0)
-    place = jnp.where(named, dot(lower, jnp.where(named, 1.0, 0.0)), 0.0)
+            core_stage(n - 1)
+        down_part(2 * n + 1, yf[n % 2])
+        if n:
+            cut_stage(n - 1)
+    core_stage(len(order) - 1)
+
     logits = total * inv
     top = jnp.max(jnp.where(named_t, logits, -jnp.inf), axis=0, keepdims=True)
     raised = jnp.where(named_t, jnp.exp(jnp.where(named_t, logits - top, 0.0)), 0.0)
@@ -455,17 +475,16 @@
 
     def share_of(expert, contribution):
         weight = jnp.sum(jnp.where(r0 == r1, jnp.sum(jnp.where(e_iota == expert, gates, 0.0), axis=0, keepdims=True), 0.0), axis=1, keepdims=True)
-        column = jnp.sum(jnp.where(lane == expert, place, 0.0), axis=1, keepdims=True)
+        column = jnp.sum(jnp.where(r0 == r1, place_row(expert), 0.0), axis=1, keepdims=True)
         return weight * dot(jnp.where(column == spot, 1.0, 0.0).astype(BF16), contribution)
 
     mixed = hid[...]
-    for j in (1, 2, 3):
-        if j == 3:
-            finish(0)
-            mixed = mixed + share_of(z, yzs[0])
+    for j in (3, 2, 1):
         plane = partner(z, j)
         remote(yzs.at[j], yzr.at[j], yz_s.at[j], yz_r.at[j], unit(plane, c), x).wait_recv()
         mixed = mixed + share_of(plane, yzr[j])
+    cut_stage(len(order) - 1)
+    mixed = mixed + share_of(z, yzs[0])
     done = mixed.astype(BF16)
     fin[0] = done
     last = send(fin.at[0], fin.at[1], f_s, f_r, u, ox)
@@ -476,7 +495,7 @@
         copy.wait_send()
 
 
-def layer(query, new_key, new_value, lengths, residual, gain, router_t, ids, ids_t, key_cache, value_cache, out_w, gate_w, up_w, down_w):
+def layer(query, new_key, new_value, lengths, residual, gain, router_t, ids_t, key_cache, value_cache, out_w, gate_w, up_w, down_w):
     rows = residual.shape[0]
     block = residual.shape[1]
     half = block // CUTS
@@ -489,7 +508,7 @@
     return pl.pallas_call(
         layer_kernel,
         out_shape=jax.ShapeDtypeStruct((rows, block), BF16),
-        in_specs=[vmem] * 3 + [pl.BlockSpec(memory_space=pltpu.SMEM)] + [vmem] * 5 + [hbm] * 6,
+        in_specs=[vmem] * 3 + [pl.BlockSpec(memory_space=pltpu.SMEM)] + [vmem] * 4 + [hbm] * 6,
         out_specs=vmem,
         scratch_shapes=[
             pltpu.VMEM(out_w.shape, BF16),
@@ -497,7 +516,7 @@
             pltpu.VMEM((W_SLOTS, block, hidden_units), BF16),
             pltpu.VMEM((D_SLOTS, hidden_units, block), BF16),
             pltpu.VMEM((query.shape[0], query.shape[1] // HD, HD), F32),
-            pltpu.VMEM((query.shape[0], query.shape[1] // HD, HD), F32),
+            pltpu.VMEM((2, query.shape[0], query.shape[1] // HD // 2, HD), F32),
             pltpu.VMEM(new_key.shape, F32),
             pltpu.VMEM(new_value.shape, F32),
             pltpu.VMEM((rows, query.shape[1]), BF16),
@@ -509,7 +528,6 @@
             pltpu.VMEM((cap, hidden_units), F32),
             pltpu.VMEM((cap, hidden_units), F32),
             pltpu.VMEM((cap, hidden_units), BF16),
-            pltpu.VMEM((cap, block), F32),
             pltpu.VMEM((PLANES, cap, block), BF16),
             pltpu.VMEM((PLANES, cap, block), BF16),
             pltpu.VMEM((PLANES, cap, half), BF16),
@@ -519,8 +537,8 @@
             pltpu.VMEM((2, rows, half), BF16),
             pltpu.VMEM((8, rows), F32),
             pltpu.VMEM((count, 8, rows), F32),
-            dma(()), dma((W_SLOTS,)), dma((W_SLOTS,)), dma((D_SLOTS,)), dma((D_SLOTS, 4)),
-            dma((4,)), dma((4,)), dma((4,)), dma((4,)), dma(()), dma(()),
+            dma(()), dma((W_SLOTS,)), dma((W_SLOTS,)), dma((D_SLOTS,)), dma((D_SLOTS, 8)),
+            dma((8,)), dma((8,)), dma((8,)), dma((8,)), dma(()), dma(()),
             dma((4,)), dma((4,)), dma((4,)), dma((4,)), dma((8,)), dma((8,)),
             dma((count,)), dma((count,)),
             dma((4,)), dma((4,)), dma((4,)), dma((4,)), dma((4,)), dma((4,)),
@@ -530,7 +548,7 @@
             collective_id=0, has_side_effects=True, vmem_limit_bytes=VMEM_MIB * 2**20
         ),
         name="layer",
-    )(query, new_key, new_value, lengths, residual, gain, router_t, ids, ids_t, key_cache, value_cache, out_w, gate_w, up_w, down_w)
+    )(query, new_key, new_value, lengths, residual, gain, router_t, ids_t, key_cache, value_cache, out_w, gate_w, up_w, down_w)
 
 
 VMEM_MIB = 62
@@ -540,9 +558,8 @@
     residual, query, key_cache, value_cache, new_key, new_value, lengths, out_weight,
     router_weight, norm_gain, expert_ids, gate_weight, up_weight, down_weight,
 ):
-    router_t = jnp.pad(router_weight.T, ((0, 8 - EXPERTS), (0, 0)))
     return layer(
-        query, new_key, new_value, lengths, residual, norm_gain[None, :], router_t, expert_ids, expert_ids.T,
+        query, new_key, new_value, lengths, residual, norm_gain, router_weight.T, expert_ids.T,
         key_cache, value_cache, out_weight, gate_weight, up_weight, down_weight,
     )
 

time: 81.2 us -> 77.6 us (0.956)
  local copies, waits for them, and re-layouts: 5.62 us -> 1.62 us
    unnamed x2 -> x1, local copies, waits for them, and re-layouts: 3.03 us -> 1.62 us
    pad x1 -> x0, local copies, waits for them, and re-layouts: 1.31 us -> none  [fused_shards(): router_t = jnp.pad(router_weight.T, ((0, 8 - EXPERTS), (0, 0)))]
    broadcast_in_dim x1 -> x0, local copies, waits for them, and re-layouts: 1.28 us -> none  [fused_shards(): norm_gain[None, :]]
where the time goes in v3:
time: 77.6 us; the launch traced here: 77.4 us
  Pallas kernels  75.8 us (98%)
  local copies, waits for them, and re-layouts  1.62 us (2%)
    pallas_call x1, Pallas kernels, layer(): pl.pallas_call(layer_kernel, out_shape=jax.ShapeDtypeStruct((rows, block)...  75.8 us
    unnamed x1, local copies, waits for them, and re-layouts  1.62 us

profile of v3, /device:TPU:0, one launch (start us, length us, event | category | flops | bytes accessed | tf_op | source)
XLA Modules:
  0.0 77.4 jit_solution(16113030773726157138)
XLA Ops:
  0.0 75.8 %layer.1 = bf16[128,768]{1,0:T(8,128)(2,1)} custom-call(bf16[16,3072]{1,0:T(8,128)(2,1)} %query.1, bf16[16,512]{1,0:T(8,128)(2,1)} %new_key.1, bf16[16,512]{1,0:T(8,128)(2,1)} %new_value.1, s32[16]{0:T(128)} %lengths.1, bf16[128,768]{1,0:T(8,128)(2,1)} %residual.1, f32[768]{0:T(1024)} %gain.1, f32[4,768]{1,0:T(4,128)} %bitcast.2, s32[2,128]{1,0:T(2,128)} %bitcast.3, ...), custom_call_target="tpu_custom_call" | custom-call | tf_op jit(solution)/shard_map/layer/pallas_call | solution.py:508
  75.8 1.6 %copy.16 = bf16[128,768]{1,0:T(8,128)(2,1)} copy(bf16[128,768]{1,0:T(8,128)(2,1)} %layer.1) | data formatting | bytes 393216

commit v4 on v3

--- a/solution.py
+++ b/solution.py
@@ -247,11 +247,12 @@
             scores = dot(q.astype(BF16), keys, ((1,), (1,))) * HD ** (-0.5)
             own = jnp.sum(q * nk[pl.ds(row, 1), here], axis=1, keepdims=True) * HD ** (-0.5)
             valid = slot_iota < lengths[row]
-            highest = jnp.maximum(jnp.max(jnp.where(valid, scores, -jnp.inf), axis=1, keepdims=True), own)
-            weights = jnp.where(valid, jnp.exp(jnp.where(valid, scores - highest, 0.0)), 0.0)
+            scores = jnp.where(valid, scores, -jnp.inf)
+            highest = jnp.maximum(jnp.max(scores, axis=1, keepdims=True), own)
+            weights = jnp.exp(scores - highest)
             own_weight = jnp.exp(own - highest)
             all_weight = jnp.sum(weights, axis=1, keepdims=True) + own_weight
-            probs = (weights / all_weight).astype(BF16)
+            probs = (weights * (1.0 / all_weight)).astype(BF16)
             own_prob = (own_weight / all_weight).astype(BF16).astype(F32)
             mix = dot(probs, values) + own_prob * nv[pl.ds(row, 1), here]
             mix = jnp.where(own_head, mix, 0.0)
@@ -441,17 +442,17 @@
             down_copy(k + D_SLOTS).start()
 
     order = (3, 2, 1, 0)
-    yf = [acc.at[:, pl.ds(0, block)] for acc in (accg, accu)]
+    yf = [acc.at[:, pl.ds(n * block, block)] for acc in (accg, accu) for n in (0, 1)]
 
     def core_stage(n):
         j = order[n]
         remote(ycs.at[j], ycr.at[j], yc_s.at[j], yc_r.at[j], unit(z, oc), x).wait_recv()
-        yxs[j] = (yf[n % 2][:, half_of(ox)] + ycr[j, :, half_of(ox)].astype(F32)).astype(BF16)
+        yxs[j] = (yf[n][:, half_of(ox)] + ycr[j, :, half_of(ox)].astype(F32)).astype(BF16)
         send(yxs.at[j], yxr.at[j], yx_s.at[j], yx_r.at[j], u, ox)
 
     def cut_stage(n):
         j = order[n]
-        mine = yf[n % 2][:, half_of(x)] + ycr[j, :, half_of(x)].astype(F32)
+        mine = yf[n][:, half_of(x)] + ycr[j, :, half_of(x)].astype(F32)
         remote(yxs.at[j], yxr.at[j], yx_s.at[j], yx_r.at[j], u, ox).wait_recv()
         yzs[j] = (mine + yxr[j].astype(F32)).astype(BF16)
         if j:
@@ -462,10 +463,11 @@
         send(ycs.at[j], ycr.at[j], yc_s.at[j], yc_r.at[j], unit(z, oc), x)
         if n:
             core_stage(n - 1)
-        down_part(2 * n + 1, yf[n % 2])
-        if n:
-            cut_stage(n - 1)
+        down_part(2 * n + 1, yf[n])
+        if n > 1:
+            cut_stage(n - 2)
     core_stage(len(order) - 1)
+    cut_stage(len(order) - 2)
 
     logits = total * inv
     top = jnp.max(jnp.where(named_t, logits, -jnp.inf), axis=0, keepdims=True)
@@ -480,11 +482,12 @@
 
     mixed = hid[...]
     for j in (3, 2, 1):
+        if j == 1:
+            cut_stage(len(order) - 1)
+            mixed = mixed + share_of(z, yzs[0])
         plane = partner(z, j)
         remote(yzs.at[j], yzr.at[j], yz_s.at[j], yz_r.at[j], unit(plane, c), x).wait_recv()
         mixed = mixed + share_of(plane, yzr[j])
-    cut_stage(len(order) - 1)
-    mixed = mixed + share_of(z, yzs[0])
     done = mixed.astype(BF16)
     fin[0] = done
     last = send(fin.at[0], fin.at[1], f_s, f_r, u, ox)

time: 77.6 us -> 73.3 us (0.945)
  Pallas kernels: 75.8 us -> 71.5 us
    pallas_call x1, Pallas kernels: 75.8 us -> 71.5 us  [layer(): pl.pallas_call(layer_kernel, out_shape=jax.ShapeDtypeStruct((rows, block)...]
where the time goes in v4:
time: 73.3 us; the launch traced here: 73.2 us
  Pallas kernels  71.5 us (98%)
  local copies, waits for them, and re-layouts  1.62 us (2%)
    pallas_call x1, Pallas kernels, layer(): pl.pallas_call(layer_kernel, out_shape=jax.ShapeDtypeStruct((rows, block)...  71.5 us
    unnamed x1, local copies, waits for them, and re-layouts  1.62 us

profile of v4, /device:TPU:0, one launch (start us, length us, event | category | flops | bytes accessed | tf_op | source)
XLA Modules:
  0.0 73.2 jit_solution(12509099392241840599)
XLA Ops:
  0.0 71.5 %layer.1 = bf16[128,768]{1,0:T(8,128)(2,1)} custom-call(bf16[16,3072]{1,0:T(8,128)(2,1)} %query.1, bf16[16,512]{1,0:T(8,128)(2,1)} %new_key.1, bf16[16,512]{1,0:T(8,128)(2,1)} %new_value.1, s32[16]{0:T(128)} %lengths.1, bf16[128,768]{1,0:T(8,128)(2,1)} %residual.1, f32[768]{0:T(1024)} %gain.1, f32[4,768]{1,0:T(4,128)} %bitcast.2, s32[2,128]{1,0:T(2,128)} %bitcast.3, ...), custom_call_target="tpu_custom_call" | custom-call | tf_op jit(solution)/shard_map/layer/pallas_call | solution.py:511
  71.5 1.6 %copy.16 = bf16[128,768]{1,0:T(8,128)(2,1)} copy(bf16[128,768]{1,0:T(8,128)(2,1)} %layer.1) | data formatting | bytes 393216
